TPU v7x, 32 devices: a whole 2x2x4 slice. The times are simulated.
32 devices in a mesh: row: 4 (over y, x), col: 8 (over z, core).
Axes of the slice: x: 2, y: 2, z: 4, core: 2. Of those that a mesh axis runs over, the one named last changes fastest.
Arguments:
- right_side: float32 [8, 512, 512], P('col', 'row'), may hold values from -6 to 6
- affinity_blocks: float32 [8, 8, 8, 128, 128], P('row', 'col'), may hold values from -0.046875 to 0.046875
- block_coords: int32 [8, 8, 8, 2], P('row', 'col'), may hold values from 0 to 3
- block_counts: int32 [8, 8], P('row', 'col'), may hold values from 4 to 8, as said below
Outputs:
- ranking: float32 [8, 512, 512], P('col', 'row')
- residual: float32 [8, 512, 512], P('col', 'row')
Inputs may be any that keep to these rules, and one draw needn't show every extreme that they name: `block_counts`: some grid tile holds 8 live blocks in every draw.
All inputs are finite; a program needn't handle non-finite values.
Results may differ from a plain program's by a relative error of at most 0.0003.
Values sent between devices are 32-bit elements; how exact they have to be, the bound alone decides.
A program may use at most 64 MiB of HBM per device.

v0:
```python
import jax
import jax.numpy as jnp
from jax import lax
from jax.sharding import PartitionSpec as P

ITERS = 3


diffusion = 0.8


def broadcast(value, axis, source):
    kept = jnp.where(lax.axis_index(axis) == source, value, 0).astype(value.dtype)
    return lax.psum(kept, axis)


def live_blocks(blocks, count):
    live = (jnp.arange(blocks.shape[0], dtype=jnp.int32) < count).astype(blocks.dtype)
    return blocks * live[:, None, None]


def forward_only(masked, rows, cols, column_field):
    position = jnp.arange(column_field.shape[0], dtype=jnp.int32)
    picked = jnp.take(column_field, cols, axis=0)
    product = jnp.einsum("kab,kbw->kaw", masked, picked, precision=lax.Precision.HIGHEST)
    row_onehot = (rows[None, :] == position[:, None]).astype(jnp.float32)
    return jnp.einsum("tk,kaw->taw", row_onehot, product, precision=lax.Precision.HIGHEST)


def backward_only(masked, rows, cols, row_field):
    position = jnp.arange(row_field.shape[0], dtype=jnp.int32)
    chosen = jnp.take(row_field, rows, axis=0)
    mirrored = jnp.einsum("kab,kaw->kbw", masked, chosen, precision=lax.Precision.HIGHEST)
    col_onehot = (cols[None, :] == position[:, None]).astype(jnp.float32)
    return jnp.einsum("tk,kbw->tbw", col_onehot, mirrored, precision=lax.Precision.HIGHEST)


def tile_products(masked, rows, cols, column_field, row_field):
    forward = forward_only(masked, rows, cols, column_field)
    backward = backward_only(masked, rows, cols, row_field)
    return (forward, backward)


def block_products(affinity_blocks, block_coords, block_counts, column_block, row_blocks):
    members = affinity_blocks.shape[0]
    edge = affinity_blocks.shape[-1]
    width = column_block.shape[1]
    column_field = column_block.reshape(-1, edge, width)
    forward_parts = []
    backward_total = jnp.zeros(column_field.shape, jnp.float32)
    for member in range(members):
        masked = live_blocks(affinity_blocks[member, 0], block_counts[member, 0])
        forward, backward = tile_products(
            masked,
            block_coords[member, 0, :, 0],
            block_coords[member, 0, :, 1],
            column_field,
            row_blocks[member].reshape(column_field.shape),
        )
        forward_parts.append(forward.reshape(column_block.shape))
        backward_total = backward_total + backward
    return (jnp.stack(forward_parts), backward_total.reshape(column_block.shape))


def operate(piece, affinity_blocks, block_coords, block_counts):
    rows_count = lax.axis_size("row")
    cols_count = lax.axis_size("col")
    members = cols_count // rows_count
    my_row = lax.axis_index("row")
    share = piece.shape[1]
    width = piece.shape[2]
    sliver = share // cols_count
    whole = lax.all_gather(piece, "row", axis=1, tiled=True)
    received = []
    for member in range(members):
        received.append(broadcast(whole[0], "col", my_row * members + member))
    row_blocks = jnp.stack(received)
    forward, backward = block_products(
        affinity_blocks, block_coords, block_counts, whole[0], row_blocks
    )
    back_part = lax.psum_scatter(backward[None], "row", scatter_dimension=1, tiled=True)
    spread = forward.reshape(members, rows_count, cols_count, sliver, width)
    summed = lax.psum_scatter(spread, "col", scatter_dimension=2, tiled=True)
    ordered = summed.reshape(members, rows_count, sliver, width).transpose(1, 0, 2, 3)
    ordered = ordered.reshape(rows_count * members, sliver, width)
    forward_part = lax.all_to_all(
        lax.all_to_all(ordered, "row", split_axis=0, concat_axis=0, tiled=True),
        "col",
        split_axis=0,
        concat_axis=1,
        tiled=True,
    )
    return piece - diffusion * (forward_part + back_part)


def squares(residual):
    return lax.psum(jnp.sum(residual * residual, axis=(0, 1)), ("row", "col"))


def shards(right_side, affinity_blocks, block_coords, block_counts):
    ranking = jnp.zeros_like(right_side)
    residual = right_side
    direction = right_side
    norm_now = squares(residual)
    for step in range(ITERS):
        image = operate(direction, affinity_blocks, block_coords, block_counts)
        curve = lax.psum(jnp.sum(direction * image, axis=(0, 1)), ("row", "col"))
        alpha = norm_now / curve
        ranking = ranking + alpha * direction
        residual = residual - alpha * image
        if step + 1 < ITERS:
            norm_next = squares(residual)
            direction = residual + norm_next / norm_now * direction
            norm_now = norm_next
    return (ranking, residual)


def solution(mesh):
    in_specs = (
        P("col", "row", None),
        P("row", "col", None, None, None),
        P("row", "col", None, None),
        P("row", "col"),
    )
    out_specs = (P("col", "row", None), P("col", "row", None))
    return jax.shard_map(shards, mesh=mesh, in_specs=in_specs, out_specs=out_specs, check_vma=False)
```

profile of v0, /device:TPU:1, one launch (start us, length us, event | category | flops | bytes accessed | tf_op | source)
XLA Modules:
  0.0 731.5 jit_solution(17342611776292399714)
XLA Ops:
  12.1 26.5 %all-gather.4.cloned.1.call-done = f32[1,512,512]{2,1,0:T(8,128)} async-done(((f32[1,128,512]{2,1,0:T(8,128)}), f32[1,512,512]{2,1,0:T(8,128)}) %all-gather.4.cloned.1.call-update) | async-done | bytes 1048592 | tf_op jit(solution)/shard_map/all_gather | solution.py:73
  38.6 3.3 gather_fusion.1
  43.6 3.6 fusion.44
  47.2 2.2 fusion.20
  51.8 3.6 fusion.46
  55.4 2.2 fusion.22
  59.8 47.7 %all-reduce.12.cloned.1.call-done = (f32[4,128,512]{2,1,0:T(8,128)}, f32[4,128,512]{2,1,0:T(8,128)}) async-done(((f32[4,128,512]{2,1,0:T(8,128)}, f32[4,128,512]{2,1,0:T(8,128)}), (f32[4,128,512]{2,1,0:T(8,128)}, f32[4,128,512]{2,1,0:T(8,128)})) %all-reduce.12.cloned.1.call-update) | async-done | bytes 2097168 | tf_op jit(solution)/shard_map/psum | solution.py:14
  107.5 3.2 gather_fusion.3
  112.6 3.7 fusion.40
  116.4 2.2 fusion.16
  120.7 2.3 fusion.48
  124.4 19.2 %reduce-scatter.7.cloned.1.call-done = f32[2,4,1,16,512]{4,3,0,1,2:T(8,128)} async-done(((f32[2,4,8,16,512]{4,3,0,1,2:T(8,128)}), f32[2,4,1,16,512]{4,3,0,1,2:T(8,128)}) %reduce-scatter.7.cloned.1.call-update) | async-done | bytes 262160 | tf_op jit(solution)/shard_map/reduce_scatter | solution.py:83
  143.6 8.7 %all_to_all.51 = f32[8,16,512]{2,1,0:T(8,128)} all-to-all(f32[8,16,512]{2,1,0:T(8,128)} %bitcast.154), channel_id=1, replica_groups=mesh['row'=4,'col'=8] {'row'}, dimensions={0} | all-to-all | bytes 524288 | tf_op jit(solution)/shard_map/all_to_all | solution.py:87
  152.3 7.8 %all-to-all-start.1 = ((f32[8,16,512]{2,1,0:T(8,128)}), f32[8,16,512]{2,1,0:T(8,128)S(1)}, u32[]{:S(2)}, u32[]{:S(2)}) async-start(f32[8,16,512]{2,1,0:T(8,128)} %all_to_all.51), calls=%async_computation.2 | async-start | bytes 524288 | tf_op jit(solution)/shard_map/all_to_all | solution.py:86
  160.1 15.2 %reduce-scatter.9.cloned.1.call-done = f32[1,128,512]{2,1,0:T(8,128)} async-done(((f32[1,512,512]{2,1,0:T(8,128)}), f32[1,128,512]{2,1,0:T(8,128)}) %reduce-scatter.9.cloned.1.call-update) | async-done | bytes 262160 | tf_op jit(solution)/shard_map/reduce_scatter | solution.py:81
  176.3 38.5 %all-reduce = (f32[512]{0:T(512)S(1)}, f32[512]{0:T(512)S(1)}) all-reduce(f32[512]{0:T(512)S(1)} %get-tuple-element.4, f32[512]{0:T(512)S(1)} %get-tuple-element.3), channel_id=1, replica_groups=mesh['row'=4,'col'=8] {'row','col'}, use_global_device_ids=true, to_apply=%region_1.0 | all-reduce | flops 1024 | bytes 8192 | tf_op jit(solution)/shard_map/psum | solution.py:97
  215.9 41.0 %psum.88 = f32[512]{0:T(512)S(1)} all-reduce(f32[512]{0:T(512)S(1)} %get-tuple-element.15), channel_id=1, replica_groups=mesh['row'=4,'col'=8] {'row','col'}, use_global_device_ids=true, to_apply=%region_9.11 | all-reduce | flops 512 | bytes 4096 | tf_op jit(solution)/shard_map/psum | solution.py:97
  258.1 26.9 %all-gather.6.cloned.1.call-done = f32[1,512,512]{2,1,0:T(8,128)} async-done(((f32[1,128,512]{2,1,0:T(8,128)}), f32[1,512,512]{2,1,0:T(8,128)}) %all-gather.6.cloned.1.call-update) | async-done | bytes 1048592 | tf_op jit(solution)/shard_map/all_gather | solution.py:73
  285.1 3.3 gather_fusion.5
  290.4 4.9 fusion.36
  297.1 3.9 fusion.12
  303.3 2.2 fusion.14
  307.6 53.3 %all-reduce.10.cloned.1.call-done = (f32[4,128,512]{2,1,0:T(8,128)}, f32[4,128,512]{2,1,0:T(8,128)}) async-done(((f32[4,128,512]{2,1,0:T(8,128)}, f32[4,128,512]{2,1,0:T(8,128)}), (f32[4,128,512]{2,1,0:T(8,128)}, f32[4,128,512]{2,1,0:T(8,128)})) %all-reduce.10.cloned.1.call-update) | async-done | bytes 2097168 | tf_op jit(solution)/shard_map/psum | solution.py:14
  360.9 3.2 gather_fusion.7
  366.1 3.7 fusion.32
  369.8 2.2 fusion.8
  374.2 2.3 fusion.51
  377.8 19.3 %reduce-scatter.11.cloned.1.call-done = f32[2,4,1,16,512]{4,3,0,1,2:T(8,128)} async-done(((f32[2,4,8,16,512]{4,3,0,1,2:T(8,128)}), f32[2,4,1,16,512]{4,3,0,1,2:T(8,128)}) %reduce-scatter.11.cloned.1.call-update) | async-done | bytes 262160 | tf_op jit(solution)/shard_map/reduce_scatter | solution.py:83
  397.1 8.7 %all_to_all.52 = f32[8,16,512]{2,1,0:T(8,128)} all-to-all(f32[8,16,512]{2,1,0:T(8,128)} %bitcast.156), channel_id=1, replica_groups=mesh['row'=4,'col'=8] {'row'}, dimensions={0} | all-to-all | bytes 524288 | tf_op jit(solution)/shard_map/all_to_all | solution.py:87
  405.8 7.9 %all-to-all-start.3 = ((f32[8,16,512]{2,1,0:T(8,128)}), f32[8,16,512]{2,1,0:T(8,128)S(1)}, u32[]{:S(2)}, u32[]{:S(2)}) async-start(f32[8,16,512]{2,1,0:T(8,128)} %all_to_all.52), calls=%async_computation.6 | async-start | bytes 524288 | tf_op jit(solution)/shard_map/all_to_all | solution.py:86
  413.6 15.6 %reduce-scatter.13.cloned.1.call-done = f32[1,128,512]{2,1,0:T(8,128)} async-done(((f32[1,512,512]{2,1,0:T(8,128)}), f32[1,128,512]{2,1,0:T(8,128)}) %reduce-scatter.13.cloned.1.call-update) | async-done | bytes 262160 | tf_op jit(solution)/shard_map/reduce_scatter | solution.py:81
  430.3 38.5 %psum.91 = f32[512]{0:T(512)S(1)} all-reduce(f32[512]{0:T(512)S(1)} %multiply_reduce_fusion.2), channel_id=1, replica_groups=mesh['row'=4,'col'=8] {'row','col'}, use_global_device_ids=true, to_apply=%region_15.17 | all-reduce | flops 512 | bytes 4096 | tf_op jit(solution)/shard_map/psum | solution.py:107
  469.9 41.0 %psum.92 = f32[512]{0:T(512)S(1)} all-reduce(f32[512]{0:T(512)S(1)} %get-tuple-element.13), channel_id=1, replica_groups=mesh['row'=4,'col'=8] {'row','col'}, use_global_device_ids=true, to_apply=%region_17.19 | all-reduce | flops 512 | bytes 4096 | tf_op jit(solution)/shard_map/psum | solution.py:97
  511.9 27.1 %all-gather.8.cloned.1.call-done = f32[1,512,512]{2,1,0:T(8,128)} async-done(((f32[1,128,512]{2,1,0:T(8,128)}), f32[1,512,512]{2,1,0:T(8,128)}) %all-gather.8.cloned.1.call-update) | async-done | bytes 1048592 | tf_op jit(solution)/shard_map/all_gather | solution.py:73
  539.0 3.3 gather_fusion.9
  544.4 4.9 fusion.28
  552.5 2.2 fusion.4
  557.1 2.2 fusion.6
  561.5 53.4 %all-reduce.8.cloned.1.call-done = (f32[4,128,512]{2,1,0:T(8,128)}, f32[4,128,512]{2,1,0:T(8,128)}) async-done(((f32[4,128,512]{2,1,0:T(8,128)}, f32[4,128,512]{2,1,0:T(8,128)}), (f32[4,128,512]{2,1,0:T(8,128)}, f32[4,128,512]{2,1,0:T(8,128)})) %all-reduce.8.cloned.1.call-update) | async-done | bytes 2097168 | tf_op jit(solution)/shard_map/psum | solution.py:14
  614.9 3.2 gather_fusion.11
  620.0 3.7 fusion.24
  623.8 2.2 fusion
  628.1 2.3 fusion.54
  631.8 19.2 %reduce-scatter.15.cloned.1.call-done = f32[2,4,1,16,512]{4,3,0,1,2:T(8,128)} async-done(((f32[2,4,8,16,512]{4,3,0,1,2:T(8,128)}), f32[2,4,1,16,512]{4,3,0,1,2:T(8,128)}) %reduce-scatter.15.cloned.1.call-update) | async-done | bytes 262160 | tf_op jit(solution)/shard_map/reduce_scatter | solution.py:83
  651.0 8.7 %all_to_all.53 = f32[8,16,512]{2,1,0:T(8,128)} all-to-all(f32[8,16,512]{2,1,0:T(8,128)} %bitcast.155), channel_id=1, replica_groups=mesh['row'=4,'col'=8] {'row'}, dimensions={0} | all-to-all | bytes 524288 | tf_op jit(solution)/shard_map/all_to_all | solution.py:87
  659.7 7.7 %all-to-all-start.5 = ((f32[8,16,512]{2,1,0:T(8,128)}), f32[8,16,512]{2,1,0:T(8,128)S(1)}, u32[]{:S(2)}, u32[]{:S(2)}) async-start(f32[8,16,512]{2,1,0:T(8,128)} %all_to_all.53), calls=%async_computation.10 | async-start | bytes 524288 | tf_op jit(solution)/shard_map/all_to_all | solution.py:86
  667.4 15.2 %reduce-scatter.17.cloned.1.call-done = f32[1,128,512]{2,1,0:T(8,128)} async-done(((f32[1,512,512]{2,1,0:T(8,128)}), f32[1,128,512]{2,1,0:T(8,128)}) %reduce-scatter.17.cloned.1.call-update) | async-done | bytes 262160 | tf_op jit(solution)/shard_map/reduce_scatter | solution.py:81
  683.7 38.5 %psum.95 = f32[512]{0:T(512)S(1)} all-reduce(f32[512]{0:T(512)S(1)} %multiply_reduce_fusion), channel_id=1, replica_groups=mesh['row'=4,'col'=8] {'row','col'}, use_global_device_ids=true, to_apply=%region_23.25 | all-reduce | flops 512 | bytes 4096 | tf_op jit(solution)/shard_map/psum | solution.py:107
  (99 shorter events, 54.5 us)
Async XLA Ops:
  7.2 31.4 %all-gather.4.cloned.1.call-start = ((), (), s32[]{:S(2)}) async-start(), calls=%async_computation.12 | async-start | bytes 1310720 | tf_op jit(solution)/shard_map/all_gather | solution.py:73
  7.9 99.6 %all-reduce.12.cloned.1.call-start = ((), (), s32[]{:S(2)}) async-start(), calls=%async_computation.23 | async-start | bytes 4194304 | tf_op jit(solution)/shard_map/psum | solution.py:14
  38.6 3.3 copy-start.1
  41.9 1.7 copy-start
  43.6 100.0 %reduce-scatter.7.cloned.1.call-start = ((), (), s32[]{:S(2)}) async-start(), calls=%async_computation.13 | async-start | bytes 2359296 | tf_op jit(solution)/shard_map/reduce_scatter | solution.py:83
  59.5 115.7 %reduce-scatter.9.cloned.1.call-start = ((), (), s32[]{:S(2)}) async-start(), calls=%async_computation.14 | async-start | bytes 1310720 | tf_op jit(solution)/shard_map/reduce_scatter | solution.py:81
  123.1 52.2 %copy-start.8 = (f32[1,128,512]{2,1,0:T(8,128)S(1)}, f32[1,128,512]{2,1,0:T(8,128)}, u32[]{:S(2)}) copy-start(f32[1,128,512]{2,1,0:T(8,128)} %param.6) | copy-start | bytes 786436
  152.3 23.0 %all-to-all-start.1 = ((f32[8,16,512]{2,1,0:T(8,128)}), f32[8,16,512]{2,1,0:T(8,128)S(1)}, u32[]{:S(2)}, u32[]{:S(2)}) async-start(f32[8,16,512]{2,1,0:T(8,128)} %all_to_all.51), calls=%async_computation.2 | async-start | bytes 524288 | tf_op jit(solution)/shard_map/all_to_all | solution.py:86
  160.1 125.0 %all-gather.6.cloned.1.call-start = ((), (), s32[]{:S(2)}) async-start(), calls=%async_computation.15 | async-start | bytes 1310720 | tf_op jit(solution)/shard_map/all_gather | solution.py:73
  257.7 103.2 %all-reduce.10.cloned.1.call-start = ((), (), s32[]{:S(2)}) async-start(), calls=%async_computation.22 | async-start | bytes 4194304 | tf_op jit(solution)/shard_map/psum | solution.py:14
  285.1 3.3 copy-start.3
  297.0 4.3 copy-start.6
  297.0 100.1 %reduce-scatter.11.cloned.1.call-start = ((), (), s32[]{:S(2)}) async-start(), calls=%async_computation.16 | async-start | bytes 2359296 | tf_op jit(solution)/shard_map/reduce_scatter | solution.py:83
  307.4 121.8 %reduce-scatter.13.cloned.1.call-start = ((), (), s32[]{:S(2)}) async-start(), calls=%async_computation.17 | async-start | bytes 1310720 | tf_op jit(solution)/shard_map/reduce_scatter | solution.py:81
  376.5 52.8 %copy-start.4 = (f32[1,128,512]{2,1,0:T(8,128)S(1)}, f32[1,128,512]{2,1,0:T(8,128)}, u32[]{:S(2)}) copy-start(f32[1,128,512]{2,1,0:T(8,128)} %multiply_add_fusion.2) | copy-start | bytes 786436
  405.8 23.5 %all-to-all-start.3 = ((f32[8,16,512]{2,1,0:T(8,128)}), f32[8,16,512]{2,1,0:T(8,128)S(1)}, u32[]{:S(2)}, u32[]{:S(2)}) async-start(f32[8,16,512]{2,1,0:T(8,128)} %all_to_all.52), calls=%async_computation.6 | async-start | bytes 524288 | tf_op jit(solution)/shard_map/all_to_all | solution.py:86
  413.6 125.4 %all-gather.8.cloned.1.call-start = ((), (), s32[]{:S(2)}) async-start(), calls=%async_computation.18 | async-start | bytes 1310720 | tf_op jit(solution)/shard_map/all_gather | solution.py:73
  469.9 69.2 %copy-start.11 = (f32[1,128,512]{2,1,0:T(8,128)}, f32[1,128,512]{2,1,0:T(8,128)S(1)}, u32[]{:S(2)}) copy-start(f32[1,128,512]{2,1,0:T(8,128)S(1)} %get-tuple-element.14) | copy-start | bytes 786436
  511.6 103.3 %all-reduce.8.cloned.1.call-start = ((), (), s32[]{:S(2)}) async-start(), calls=%async_computation.21 | async-start | bytes 4194304 | tf_op jit(solution)/shard_map/psum | solution.py:14
  539.0 3.3 copy-start.2
  550.9 1.6 copy-start.7
  551.0 100.1 %reduce-scatter.15.cloned.1.call-start = ((), (), s32[]{:S(2)}) async-start(), calls=%async_computation.19 | async-start | bytes 2359296 | tf_op jit(solution)/shard_map/reduce_scatter | solution.py:83
  552.5 2.5 copy-start.5
  561.2 121.5 %reduce-scatter.17.cloned.1.call-start = ((), (), s32[]{:S(2)}) async-start(), calls=%async_computation.20 | async-start | bytes 1310720 | tf_op jit(solution)/shard_map/reduce_scatter | solution.py:81
  630.5 52.2 %copy-start.10 = (f32[1,128,512]{2,1,0:T(8,128)S(1)}, f32[1,128,512]{2,1,0:T(8,128)}, u32[]{:S(2)}) copy-start(f32[1,128,512]{2,1,0:T(8,128)} %multiply_add_fusion.1) | copy-start | bytes 786436
  630.5 91.8 %copy-start.9 = (f32[1,128,512]{2,1,0:T(8,128)S(1)}, f32[1,128,512]{2,1,0:T(8,128)}, u32[]{:S(2)}) copy-start(f32[1,128,512]{2,1,0:T(8,128)} %param.6) | copy-start | bytes 786436
  630.5 91.8 %copy-start.12 = (f32[1,128,512]{2,1,0:T(8,128)S(1)}, f32[1,128,512]{2,1,0:T(8,128)}, u32[]{:S(2)}) copy-start(f32[1,128,512]{2,1,0:T(8,128)} %copy-done.11) | copy-start | bytes 786436
  659.7 23.0 %all-to-all-start.5 = ((f32[8,16,512]{2,1,0:T(8,128)}), f32[8,16,512]{2,1,0:T(8,128)S(1)}, u32[]{:S(2)}, u32[]{:S(2)}) async-start(f32[8,16,512]{2,1,0:T(8,128)} %all_to_all.53), calls=%async_computation.10 | async-start | bytes 524288 | tf_op jit(solution)/shard_map/all_to_all | solution.py:86
Sparse Core Ops, SparseCore 0:
  9.8 28.6 all-gather.3
  43.7 63.7 all-reduce.11
  109.8 33.7 reduce-scatter.6
  146.4 28.8 reduce-scatter.8
  257.8 27.2 all-gather.5
  297.1 63.7 all-reduce.9
  363.3 33.7 reduce-scatter.10
  400.2 28.9 reduce-scatter.12
  511.8 27.2 all-gather.7
  551.1 63.7 all-reduce.7
  617.2 33.7 reduce-scatter.14
  653.8 28.8 reduce-scatter.16
where the time goes:
time: 742 us; the launch traced here: 731 us
  waiting for transfers between devices  339 us (46%)
  blocking collectives  224 us (30%)
  matrix products  67.1 us (9%)
  local copies, waits for them, and re-layouts  40.9 us (6%)
  starting transfers between devices  25.1 us (3%)
  other arithmetic  20.3 us (3%)
  between operations  15 us (2%)
    psum x3, waiting for transfers between devices, broadcast(): return lax.psum(kept, axis)  154 us
    psum x3, blocking collectives, squares(): return lax.psum(jnp.sum(residual * residual, axis=(0, 1)), ('row', 'col'))  121 us
    all_gather x3, waiting for transfers between devices, operate(): whole = lax.all_gather(piece, 'row', axis=1, tiled=True)  80.5 us
    psum x2, blocking collectives, shards(): curve = lax.psum(jnp.sum(direction * image, axis=(0, 1)), ('row', 'col'))  77.1 us
    reduce_scatter x3, waiting for transfers between devices, operate(): summed = lax.psum_scatter(spread, 'col', scatter_dimension=2, tiled=True)  57.7 us
    reduce_scatter x3, waiting for transfers between devices, operate(): lax.psum_scatter(backward[None], 'row', scatter_dimension=1, tiled=True)  46 us
    all_to_all x3, blocking collectives, operate(): lax.all_to_all(ordered, 'row', split_axis=0, concat_axis=0, tiled=True)  26 us
    all_to_all x3, starting transfers between devices, operate(): lax.all_to_all(lax.all_to_all(ordered, 'row', split_axis=0, concat_axis=0...  23.4 us
  transfers between devices with their start and end apart: 15, of which 12 were waited for; matrix products, arithmetic and copies ran while one was open for 12% of the time, Pallas kernels for 0%

commit v1 on v0

v1 whole, which is shorter than its diff:
```python
import functools

import jax
import jax.numpy as jnp
from jax import lax
from jax.experimental import pallas as pl
from jax.experimental.pallas import tpu as pltpu
from jax.sharding import PartitionSpec as P

ITERS = 3
CHUNKS = 2
diffusion = 0.8
MESH = pl.DeviceIdType.MESH
f32 = jnp.float32
bf16 = jnp.bfloat16


def split(value):
    high = value.astype(bf16)
    return high, (value - high.astype(f32)).astype(bf16)


def kernel(R, PC, right, blocks, coords, counts, out_x, out_r, tile, thi, tlo, uhi, ulo, dcat,
           dz, dr, fw, fin, bw, rin, part, din, drow, drin, xs, rs,
           s0, s0s, sp1, sp1s, sb, sbs, sf, sfs, srs, srss, sd, sds, se, ses, so, sos):
    r = lax.axis_index("row")
    c = lax.axis_index("col")
    p = c // 2
    a = c % 2
    sibling = (r, 2 * p + 1 - a)
    edge = right.shape[1] * R
    sh = right.shape[1]
    cw = dz.shape[-1]
    blk = blocks.shape[-1]
    bt = edge // blk
    group = 2 * edge

    def remote(src, dst, send, recv, device):
        return pltpu.make_async_remote_copy(
            src_ref=src, dst_ref=dst, send_sem=send, recv_sem=recv, device_id=device, device_id_type=MESH)

    barrier = pltpu.get_barrier_semaphore()
    for j in range(1, R):
        pl.semaphore_signal(barrier, inc=1, device_id=(lax.rem(r + j, R), c), device_id_type=MESH)
    for j in range(1, PC):
        pl.semaphore_signal(barrier, inc=1, device_id=(r, 2 * lax.rem(p + j, PC) + a), device_id_type=MESH)
    pl.semaphore_signal(barrier, inc=1, device_id=sibling, device_id_type=MESH)
    pl.semaphore_wait(barrier, R + PC - 1)

    drain = []
    own = pl.ds(pl.multiple_of(r * sh, sh), sh)

    def columns(core, ch):
        return pl.ds(pl.multiple_of((core * CHUNKS + ch) * cw, 128), cw)

    first = []
    for ch in range(CHUNKS):
        copy = remote(right.at[0, :, columns(1 - a, ch)], dz.at[0, ch, a, own, :], s0s.at[ch], s0.at[ch], sibling)
        copy.start()
        first.append(copy)
        drain.append((None, copy))
        dz[0, ch, a, own, :] = right[0, :, columns(a, ch)]

    for m in range(2):
        @pl.loop(0, bt * bt)
        def _(q, m=m):
            t = q // bt
            u = q % bt
            total = jnp.zeros((blk, blk), f32)
            for k in range(blocks.shape[2]):
                live = (k < counts[m, 0]) & (coords[m, 0, k, 0] == t) & (coords[m, 0, k, 1] == u)
                total = total + jnp.where(live, 1.0, 0.0).astype(f32) * blocks[m, 0, k]
            tile[a, pl.ds(pl.multiple_of(m * edge + t * blk, blk), blk), pl.ds(pl.multiple_of(u * blk, blk), blk)] = total
    half = remote(tile.at[a], tile.at[a], s0s.at[CHUNKS], s0.at[CHUNKS], sibling)
    half.start()
    drain.append((None, half))

    def rows_of(s):
        return pl.ds(pl.multiple_of(s * sh, sh), sh)

    def send_p1(it, ch):
        for j in range(1, R):
            src = dz.at[it, ch, :, own, :]
            copy = remote(src, src, sp1s.at[it, ch, j], sp1.at[it, ch, j], (lax.rem(r + j, R), c))
            copy.start()
            drain.append((None, copy))

    up = (p >= r) & (p < PC - 1)
    down = (p <= r) & (p > 0)
    upper = (r, 2 * jnp.minimum(p + 1, PC - 1) + a)
    lower = (r, 2 * jnp.maximum(p - 1, 0) + a)

    def recv_wait(dst, sem):
        remote(dst, dst, sem, sem, sibling).wait_recv()

    def multiply(hi, lo, source, target):
        dh, dl = split(source)
        dcat[:, 0:cw] = dh
        dcat[:, cw:2 * cw] = dl
        step = 256
        per = edge // step

        @pl.loop(0, group // step)
        def _(i):
            rows = pl.ds(pl.multiple_of(i * step, step), step)
            wide = jnp.dot(hi[rows, :], dcat[...], preferred_element_type=f32)
            extra = jnp.dot(lo[rows, :], dcat[:, 0:cw], preferred_element_type=f32)
            target[i // per, pl.ds(pl.multiple_of((i % per) * step, step), step), :] = (
                wide[:, 0:cw] + (wide[:, cw:2 * cw] + extra))

    def fold(value):
        return jnp.sum(value.reshape(-1, 8, cw), axis=0)

    def reduce_start(n, ch, value):
        part[n, ch] = value
        for j in range(1, R):
            copy = remote(part.at[n, ch], din.at[n, ch, j], sds.at[n, ch, j], sd.at[n, ch, j], (lax.rem(r + j, R), c))
            copy.start()
            drain.append((None, copy))

    def reduce_middle(n, ch):
        total = part[n, ch]
        for j in range(1, R):
            recv_wait(din.at[n, ch, j], sd.at[n, ch, j])
            total = total + din[n, ch, j]
        drow[n, ch] = total
        for j in range(1, PC):
            copy = remote(drow.at[n, ch], drin.at[n, ch, j], ses.at[n, ch, j], se.at[n, ch, j],
                          (r, 2 * lax.rem(p + j, PC) + a))
            copy.start()
            drain.append((None, copy))

    def reduce_end(n, ch):
        total = drow[n, ch]
        for j in range(1, PC):
            recv_wait(drin.at[n, ch, j], se.at[n, ch, j])
            total = total + drin[n, ch, j]
        return total

    def column_sum(value):
        return jnp.sum(value, axis=0, keepdims=True)

    diag = p == r

    def stream(ch):
        first[ch].wait_recv()
        send_p1(0, ch)
        start = dz[0, ch, :, own, :]
        rs[ch] = start
        xs[ch] = jnp.zeros_like(start)
        reduce_start(0, ch, fold(start * start))
        yield
        reduce_middle(0, ch)
        rr = None
        for it in range(ITERS):
            for j in range(R):
                slot = lax.rem(r - j + R, R)
                if j > 0:
                    recv_wait(dz.at[it, ch, :, rows_of(slot), :], sp1.at[it, ch, j])

                @pl.when(diag)
                def _():
                    dr[it, ch, :, rows_of(slot), :] = dz[it, ch, :, rows_of(slot), :]
                    relay_now(it, ch, slot, j)
            if it == 0 and ch == 0:
                prepare()
            multiply(thi, tlo, dz[it, ch].reshape(group, cw), fw.at[it, ch])
            yield
            for j in range(R):
                slot = lax.rem(r - j + R, R)
                rows = rows_of(slot)

                @pl.when(p != r)
                def _():
                    recv_wait(dr.at[it, ch, :, rows, :], sb.at[it, ch, j])
                    relay_now(it, ch, slot, j)

                @pl.when(down)
                def _():
                    recv_wait(fin.at[it, ch, 0, :, rows, :], sf.at[it, ch, 0, j])
                    fw[it, ch, :, rows, :] += fin[it, ch, 0, :, rows, :]

                @pl.when(up)
                def _():
                    recv_wait(fin.at[it, ch, 1, :, rows, :], sf.at[it, ch, 1, j])
                    fw[it, ch, :, rows, :] += fin[it, ch, 1, :, rows, :]

                src = fw.at[it, ch, :, rows, :]
                cu = remote(src, fin.at[it, ch, 0, :, rows, :], sfs.at[it, ch, j], sf.at[it, ch, 0, j], upper)
                cd = remote(src, fin.at[it, ch, 1, :, rows, :], sfs.at[it, ch, j], sf.at[it, ch, 1, j], lower)
                pl.when(p < r)(cu.start)
                pl.when(p > r)(cd.start)
                drain.append((p < r, cu))
                drain.append((p > r, cd))
                for way, cond in ((0, up), (1, down)):
                    drain.append((cond, relay_copy(it, ch, slot, j, way)))
                yield
            multiply(uhi, ulo, dr[it, ch].reshape(group, cw), bw.at[it, ch])

            @pl.when(diag)
            def _():
                bw[it, ch] += fw[it, ch]
            for j in range(1, R):
                to = lax.rem(r + j, R)
                copy = remote(bw.at[it, ch, :, rows_of(to), :], rin.at[it, ch, j], srss.at[it, ch, j],
                              srs.at[it, ch, j], (to, c))
                copy.start()
                drain.append((None, copy))
            if it == 0:
                rr = column_sum(reduce_end(0, ch))
            yield
            total = bw[it, ch, :, own, :]
            for j in range(1, R):
                recv_wait(rin.at[it, ch, j], srs.at[it, ch, j])
                total = total + rin[it, ch, j]
            way = dz[it, ch, :, own, :]
            image = way - diffusion * total
            bw[it, ch, :, own, :] = image
            reduce_start(2 * it + 1, ch, fold(way * image))
            yield
            reduce_middle(2 * it + 1, ch)
            yield
            alpha = (rr / column_sum(reduce_end(2 * it + 1, ch)))[None]
            xs[ch] = xs[ch] + alpha * way
            residual = rs[ch] - alpha * bw[it, ch, :, own, :]
            rs[ch] = residual
            if it + 1 < ITERS:
                reduce_start(2 * it + 2, ch, fold(residual * residual))
                yield
                reduce_middle(2 * it + 2, ch)
                yield
                new = column_sum(reduce_end(2 * it + 2, ch))
                dz[it + 1, ch, :, own, :] = rs[ch] + (new / rr)[None] * dz[it, ch, :, own, :]
                rr = new
                send_p1(it + 1, ch)
                yield
        for n, (kept, out) in enumerate(((xs, out_x), (rs, out_r))):
            out[0, :, columns(a, ch)] = kept[ch, a]
            copy = remote(kept.at[ch, 1 - a], out.at[0, :, columns(a, ch)], sos.at[ch, n], so.at[ch, n], sibling)
            copy.start()
            drain.append((None, copy))
        yield
        for n in range(2):
            recv_wait(out_x.at[0, :, columns(1 - a, ch)], so.at[ch, n])

    def relay_copy(it, ch, slot, j, way):
        ref = dr.at[it, ch, :, rows_of(slot), :]
        return remote(ref, ref, sbs.at[it, ch, way, j], sb.at[it, ch, j], lower if way else upper)

    def relay_now(it, ch, slot, j):
        pl.when(up)(relay_copy(it, ch, slot, j, 0).start)
        pl.when(down)(relay_copy(it, ch, slot, j, 1).start)

    def prepare():
        half.wait_recv()

        @pl.loop(0, group // blk)
        def _(i):
            rows = pl.ds(pl.multiple_of(i * blk, blk), blk)
            for u in range(group // blk):
                piece = tile[u * blk // edge, rows, u * blk % edge:u * blk % edge + blk]
                thi[rows, u * blk:(u + 1) * blk], tlo[rows, u * blk:(u + 1) * blk] = split(piece)
                uhi[u * blk:(u + 1) * blk, rows], ulo[u * blk:(u + 1) * blk, rows] = split(piece.T)

    streams = [stream(ch) for ch in range(CHUNKS)]
    alive = list(streams)
    while alive:
        for item in list(alive):
            try:
                next(item)
            except StopIteration:
                alive.remove(item)
    for cond, copy in drain:
        if cond is None:
            copy.wait_send()
        else:
            pl.when(cond)(copy.wait_send)


def shards(R, PC, right_side, affinity_blocks, block_coords, block_counts):
    sh, W = right_side.shape[1:]
    edge = sh * R
    group = 2 * edge
    cw = W // 2 // CHUNKS
    N = 2 * ITERS
    dma = pltpu.SemaphoreType.DMA
    vm = pltpu.VMEM
    field = (ITERS, CHUNKS, 2, edge, cw)
    scratch = [
        vm((2, group, edge), f32),
        vm((group, group), bf16), vm((group, group), bf16), vm((group, group), bf16), vm((group, group), bf16),
        vm((group, 2 * cw), bf16),
        vm(field, f32), vm(field, f32), vm(field, f32),
        vm((ITERS, CHUNKS, 2, 2, edge, cw), f32),
        vm(field, f32),
        vm((ITERS, CHUNKS, R, 2, sh, cw), f32),
        vm((N, CHUNKS, 8, cw), f32), vm((N, CHUNKS, R, 8, cw), f32),
        vm((N, CHUNKS, 8, cw), f32), vm((N, CHUNKS, PC, 8, cw), f32),
        vm((CHUNKS, 2, sh, cw), f32), vm((CHUNKS, 2, sh, cw), f32),
        dma((CHUNKS + 1,)), dma((CHUNKS + 1,)),
        dma((ITERS, CHUNKS, R)), dma((ITERS, CHUNKS, R)),
        dma((ITERS, CHUNKS, R)), dma((ITERS, CHUNKS, 2, R)),
        dma((ITERS, CHUNKS, 2, R)), dma((ITERS, CHUNKS, R)),
        dma((ITERS, CHUNKS, R)), dma((ITERS, CHUNKS, R)),
        dma((N, CHUNKS, R)), dma((N, CHUNKS, R)),
        dma((N, CHUNKS, PC)), dma((N, CHUNKS, PC)),
        dma((CHUNKS, 2)), dma((CHUNKS, 2)),
    ]
    vmem = pl.BlockSpec(memory_space=pltpu.VMEM)
    smem = pl.BlockSpec(memory_space=pltpu.SMEM)
    out = jax.ShapeDtypeStruct(right_side.shape, f32)
    return pl.pallas_call(
        functools.partial(kernel, R, PC),
        out_shape=(out, out),
        in_specs=[vmem, vmem, smem, smem],
        out_specs=(vmem, vmem),
        scratch_shapes=scratch,
        compiler_params=pltpu.CompilerParams(
            collective_id=0, has_side_effects=True, vmem_limit_bytes=56 * 1024 * 1024),
    )(right_side, affinity_blocks, block_coords, block_counts)


def solution(mesh):
    in_specs = (
        P("col", "row", None),
        P("row", "col", None, None, None),
        P("row", "col", None, None),
        P("row", "col"),
    )
    out_specs = (P("col", "row", None), P("col", "row", None))
    R = mesh.shape["row"]
    PC = mesh.shape["col"] // 2
    return jax.shard_map(functools.partial(shards, R, PC), mesh=mesh, in_specs=in_specs, out_specs=out_specs, check_vma=False)
```

time: 742 us -> 519 us (0.70); the launches traced: 731 us -> 519 us
  Pallas kernels: 0 us -> 513 us
  waiting for transfers between devices: 339 us -> 0 us
  blocking collectives: 224 us -> 0 us
  matrix products: 67.1 us -> 0 us
  local copies, waits for them, and re-layouts: 40.9 us -> 5.08 us
  starting transfers between devices: 25.1 us -> 0 us
  other arithmetic: 20.3 us -> 0 us
  between operations: 15 us -> 0.65 us
    pallas_call x0 -> x1, Pallas kernels: none -> 513 us  [shards(): pl.pallas_call(functools.partial(kernel, R, PC), out_shape=(out, out), in...]
    psum x5 -> x0, blocking collectives: 198 us -> none  [the longest x3 121 us: squares(): return lax.psum(jnp.sum(residual * residual, axis=(0, 1)), ('row', 'col'))]
    psum x3 -> x0, waiting for transfers between devices: 154 us -> none  [broadcast(): return lax.psum(kept, axis)]
    reduce_scatter x6 -> x0, waiting for transfers between devices: 104 us -> none  [the longest x3 57.7 us: operate(): summed = lax.psum_scatter(spread, 'col', scatter_dimension=2, tiled=True)]
    all_gather x3 -> x0, waiting for transfers between devices: 80.5 us -> none  [operate(): whole = lax.all_gather(piece, 'row', axis=1, tiled=True)]
    dot_general x24 -> x0, matrix products: 67.1 us -> none  [the longest x6 21 us: forward_only(): jnp.einsum('kab,kbw->kaw', masked, picked, precision=lax.Precision.HIGHEST)]
    gather x12 -> x0, local copies, waits for them, and re-layouts: 31.4 us -> none  [the longest x6 16.1 us: forward_only(): picked = jnp.take(column_field, cols, axis=0)]
    all_to_all x3 -> x0, blocking collectives: 26 us -> none  [operate(): lax.all_to_all(ordered, 'row', split_axis=0, concat_axis=0, tiled=True)]
  transfers between devices with their start and end apart: 15 -> 0, of which waited for: 12 -> 0; matrix products, arithmetic and copies ran while one was open for 12% -> 0% of each run, Pallas kernels for 0% -> 0%
where the time goes in v1:
time: 519 us
  Pallas kernels  513 us (99%)
    pallas_call x1, Pallas kernels, shards(): pl.pallas_call(functools.partial(kernel, R, PC), out_shape=(out, out), in...  513 us

profile of v1, /device:TPU:1, one launch (start us, length us, event | category | flops | bytes accessed | tf_op | source)
XLA Modules:
  0.0 519.0 jit_solution(9900946147839426778)
XLA Ops:
  0.6 1.3 copy.7.counts
  1.9 1.4 copy.6.coords
  3.3 513.3 %shard_map.59 = (f32[1,128,512]{2,1,0:T(8,128)}, f32[1,128,512]{2,1,0:T(8,128)}) custom-call(f32[1,128,512]{2,1,0:T(8,128)} %right.1, f32[2,1,8,128,128]{4,3,2,1,0:T(8,128)} %blocks.1, s32[2,1,8,2]{3,2,1,0:T(8,128)} %copy.6.coords, s32[2,1]{1,0:T(2,128)} %copy.7.counts), custom_call_target="tpu_custom_call" | custom-call | tf_op jit(solution)/shard_map/pallas_call | solution.py:312
  516.6 0.0 copy-start
  516.6 1.7 copy.10
  518.3 0.0 copy-done
  518.3 0.7 copy.11
Async XLA Ops:
  516.6 1.7 copy-start

commit v2 on v1

--- a/solution.py
+++ b/solution.py
@@ -141,6 +141,7 @@
         return jnp.sum(value, axis=0, keepdims=True)
 
     diag = p == r
+    outermost = (p != r) & ((p == 0) | (p == PC - 1))
 
     def stream(ch):
         first[ch].wait_recv()
@@ -165,6 +166,8 @@
             if it == 0 and ch == 0:
                 prepare()
             multiply(thi, tlo, dz[it, ch].reshape(group, cw), fw.at[it, ch])
+            for j in range(R):
+                inward(it, ch, lax.rem(r - j + R, R), j, outermost)
             yield
             for j in range(R):
                 slot = lax.rem(r - j + R, R)
@@ -185,13 +188,7 @@
                     recv_wait(fin.at[it, ch, 1, :, rows, :], sf.at[it, ch, 1, j])
                     fw[it, ch, :, rows, :] += fin[it, ch, 1, :, rows, :]
 
-                src = fw.at[it, ch, :, rows, :]
-                cu = remote(src, fin.at[it, ch, 0, :, rows, :], sfs.at[it, ch, j], sf.at[it, ch, 0, j], upper)
-                cd = remote(src, fin.at[it, ch, 1, :, rows, :], sfs.at[it, ch, j], sf.at[it, ch, 1, j], lower)
-                pl.when(p < r)(cu.start)
-                pl.when(p > r)(cd.start)
-                drain.append((p < r, cu))
-                drain.append((p > r, cd))
+                inward(it, ch, slot, j, jnp.logical_not(outermost))
                 for way, cond in ((0, up), (1, down)):
                     drain.append((cond, relay_copy(it, ch, slot, j, way)))
                 yield
@@ -243,6 +240,14 @@
         for n in range(2):
             recv_wait(out_x.at[0, :, columns(1 - a, ch)], so.at[ch, n])
 
+    def inward(it, ch, slot, j, allowed):
+        src = fw.at[it, ch, :, rows_of(slot), :]
+        cu = remote(src, fin.at[it, ch, 0, :, rows_of(slot), :], sfs.at[it, ch, j], sf.at[it, ch, 0, j], upper)
+        cd = remote(src, fin.at[it, ch, 1, :, rows_of(slot), :], sfs.at[it, ch, j], sf.at[it, ch, 1, j], lower)
+        for cond, copy in (((p < r) & allowed, cu), ((p > r) & allowed, cd)):
+            pl.when(cond)(copy.start)
+            drain.append((cond, copy))
+
     def relay_copy(it, ch, slot, j, way):
         ref = dr.at[it, ch, :, rows_of(slot), :]
         return remote(ref, ref, sbs.at[it, ch, way, j], sb.at[it, ch, j], lower if way else upper)

time: 519 us -> 336 us (0.65)
  Pallas kernels: 513 us -> 330 us
    pallas_call x1, Pallas kernels: 513 us -> 330 us  [shards(): pl.pallas_call(functools.partial(kernel, R, PC), out_shape=(out, out), in...]
where the time goes in v2:
time: 336 us
  Pallas kernels  330 us (98%)
  local copies, waits for them, and re-layouts  5.08 us (2%)
    pallas_call x1, Pallas kernels, shards(): pl.pallas_call(functools.partial(kernel, R, PC), out_shape=(out, out), in...  330 us

profile of v2, /device:TPU:1, one launch (start us, length us, event | category | flops | bytes accessed | tf_op | source)
XLA Modules:
  0.0 335.7 jit_solution(8304058323772956943)
XLA Ops:
  0.6 1.3 copy.7.counts
  1.9 1.4 copy.6.coords
  3.3 329.9 %shard_map.59 = (f32[1,128,512]{2,1,0:T(8,128)}, f32[1,128,512]{2,1,0:T(8,128)}) custom-call(f32[1,128,512]{2,1,0:T(8,128)} %right.1, f32[2,1,8,128,128]{4,3,2,1,0:T(8,128)} %blocks.1, s32[2,1,8,2]{3,2,1,0:T(8,128)} %copy.6.coords, s32[2,1]{1,0:T(2,128)} %copy.7.counts), custom_call_target="tpu_custom_call" | custom-call | tf_op jit(solution)/shard_map/pallas_call | solution.py:317
  333.2 0.0 copy-start
  333.2 1.7 copy.10
  335.0 0.0 copy-done
  335.0 0.7 copy.11
Async XLA Ops:
  333.2 1.7 copy-start

commit v3 on v2

--- a/solution.py
+++ b/solution.py
@@ -60,20 +60,6 @@
         first.append(copy)
         drain.append((None, copy))
         dz[0, ch, a, own, :] = right[0, :, columns(a, ch)]
-
-    for m in range(2):
-        @pl.loop(0, bt * bt)
-        def _(q, m=m):
-            t = q // bt
-            u = q % bt
-            total = jnp.zeros((blk, blk), f32)
-            for k in range(blocks.shape[2]):
-                live = (k < counts[m, 0]) & (coords[m, 0, k, 0] == t) & (coords[m, 0, k, 1] == u)
-                total = total + jnp.where(live, 1.0, 0.0).astype(f32) * blocks[m, 0, k]
-            tile[a, pl.ds(pl.multiple_of(m * edge + t * blk, blk), blk), pl.ds(pl.multiple_of(u * blk, blk), blk)] = total
-    half = remote(tile.at[a], tile.at[a], s0s.at[CHUNKS], s0.at[CHUNKS], sibling)
-    half.start()
-    drain.append((None, half))
 
     def rows_of(s):
         return pl.ds(pl.multiple_of(s * sh, sh), sh)
@@ -169,29 +155,20 @@
             for j in range(R):
                 inward(it, ch, lax.rem(r - j + R, R), j, outermost)
             yield
+            for tick in range(R + 1):
+                if tick < R:
+                    pl.when(near)(functools.partial(outward_step, it, ch, tick))
+                    pl.when(far)(functools.partial(inward_step, it, ch, tick))
+                if tick > 0:
+                    pl.when(near)(functools.partial(inward_step, it, ch, tick - 1))
+                    pl.when(far)(functools.partial(outward_step, it, ch, tick - 1))
+                yield
             for j in range(R):
                 slot = lax.rem(r - j + R, R)
-                rows = rows_of(slot)
-
-                @pl.when(p != r)
-                def _():
-                    recv_wait(dr.at[it, ch, :, rows, :], sb.at[it, ch, j])
-                    relay_now(it, ch, slot, j)
-
-                @pl.when(down)
-                def _():
-                    recv_wait(fin.at[it, ch, 0, :, rows, :], sf.at[it, ch, 0, j])
-                    fw[it, ch, :, rows, :] += fin[it, ch, 0, :, rows, :]
-
-                @pl.when(up)
-                def _():
-                    recv_wait(fin.at[it, ch, 1, :, rows, :], sf.at[it, ch, 1, j])
-                    fw[it, ch, :, rows, :] += fin[it, ch, 1, :, rows, :]
-
-                inward(it, ch, slot, j, jnp.logical_not(outermost))
                 for way, cond in ((0, up), (1, down)):
                     drain.append((cond, relay_copy(it, ch, slot, j, way)))
-                yield
+                for way, cond in ((0, p < r), (1, p > r)):
+                    drain.append((cond, inward_copy(it, ch, slot, j, way)))
             multiply(uhi, ulo, dr[it, ch].reshape(group, cw), bw.at[it, ch])
 
             @pl.when(diag)
@@ -240,13 +217,35 @@
         for n in range(2):
             recv_wait(out_x.at[0, :, columns(1 - a, ch)], so.at[ch, n])
 
+    near = jnp.abs(p - r) <= 1
+    far = jnp.abs(p - r) > 1
+
+    def outward_step(it, ch, j):
+        slot = lax.rem(r - j + R, R)
+
+        @pl.when(p != r)
+        def _():
+            recv_wait(dr.at[it, ch, :, rows_of(slot), :], sb.at[it, ch, j])
+            relay_now(it, ch, slot, j)
+
+    def inward_step(it, ch, j):
+        slot = lax.rem(r - j + R, R)
+        rows = rows_of(slot)
+        for way, cond in ((0, down), (1, up)):
+            @pl.when(cond)
+            def _():
+                recv_wait(fin.at[it, ch, way, :, rows, :], sf.at[it, ch, way, j])
+                fw[it, ch, :, rows, :] += fin[it, ch, way, :, rows, :]
+        inward(it, ch, slot, j, jnp.logical_not(outermost))
+
+    def inward_copy(it, ch, slot, j, way):
+        src = fw.at[it, ch, :, rows_of(slot), :]
+        return remote(src, fin.at[it, ch, way, :, rows_of(slot), :], sfs.at[it, ch, j], sf.at[it, ch, way, j],
+                      lower if way else upper)
+
     def inward(it, ch, slot, j, allowed):
-        src = fw.at[it, ch, :, rows_of(slot), :]
-        cu = remote(src, fin.at[it, ch, 0, :, rows_of(slot), :], sfs.at[it, ch, j], sf.at[it, ch, 0, j], upper)
-        cd = remote(src, fin.at[it, ch, 1, :, rows_of(slot), :], sfs.at[it, ch, j], sf.at[it, ch, 1, j], lower)
-        for cond, copy in (((p < r) & allowed, cu), ((p > r) & allowed, cd)):
-            pl.when(cond)(copy.start)
-            drain.append((cond, copy))
+        pl.when((p < r) & allowed)(inward_copy(it, ch, slot, j, 0).start)
+        pl.when((p > r) & allowed)(inward_copy(it, ch, slot, j, 1).start)
 
     def relay_copy(it, ch, slot, j, way):
         ref = dr.at[it, ch, :, rows_of(slot), :]
@@ -268,6 +267,21 @@
                 uhi[u * blk:(u + 1) * blk, rows], ulo[u * blk:(u + 1) * blk, rows] = split(piece.T)
 
     streams = [stream(ch) for ch in range(CHUNKS)]
+    for item in streams:
+        next(item)
+    for m in range(2):
+        @pl.loop(0, bt * bt)
+        def _(q, m=m):
+            t = q // bt
+            u = q % bt
+            total = jnp.zeros((blk, blk), f32)
+            for k in range(blocks.shape[2]):
+                live = (k < counts[m, 0]) & (coords[m, 0, k, 0] == t) & (coords[m, 0, k, 1] == u)
+                total = total + jnp.where(live, 1.0, 0.0).astype(f32) * blocks[m, 0, k]
+            tile[a, pl.ds(pl.multiple_of(m * edge + t * blk, blk), blk), pl.ds(pl.multiple_of(u * blk, blk), blk)] = total
+    half = remote(tile.at[a], tile.at[a], s0s.at[CHUNKS], s0.at[CHUNKS], sibling)
+    half.start()
+    drain.append((None, half))
     alive = list(streams)
     while alive:
         for item in list(alive):

time: 336 us -> 211 us (0.63)
  Pallas kernels: 330 us -> 205 us
    pallas_call x1, Pallas kernels: 330 us -> 205 us  [shards(): pl.pallas_call(functools.partial(kernel, R, PC), out_shape=(out, out), in...]
where the time goes in v3:
time: 211 us
  Pallas kernels  205 us (97%)
  local copies, waits for them, and re-layouts  5.08 us (2%)
    pallas_call x1, Pallas kernels, shards(): pl.pallas_call(functools.partial(kernel, R, PC), out_shape=(out, out), in...  205 us
    unnamed x6, local copies, waits for them, and re-layouts  5.08 us

profile of v3, /device:TPU:1, one launch (start us, length us, event | category | flops | bytes accessed | tf_op | source)
XLA Modules:
  0.0 210.6 jit_solution(14434978050446423100)
XLA Ops:
  0.6 1.3 copy.7.counts
  1.9 1.4 copy.6.coords
  3.3 204.8 %shard_map.59 = (f32[1,128,512]{2,1,0:T(8,128)}, f32[1,128,512]{2,1,0:T(8,128)}) custom-call(f32[1,128,512]{2,1,0:T(8,128)} %right.1, f32[2,1,8,128,128]{4,3,2,1,0:T(8,128)} %blocks.1, s32[2,1,8,2]{3,2,1,0:T(8,128)} %copy.6.coords, s32[2,1]{1,0:T(2,128)} %copy.7.counts), custom_call_target="tpu_custom_call" | custom-call | tf_op jit(solution)/shard_map/pallas_call | solution.py:331
  208.1 0.0 copy-start
  208.1 1.7 copy.10
  209.8 0.0 copy-done
  209.8 0.7 copy.11
Async XLA Ops:
  208.1 1.7 copy-start

commit v4 on v3

--- a/solution.py
+++ b/solution.py
@@ -9,6 +9,7 @@
 
 ITERS = 3
 CHUNKS = 2
+LEAD = 3
 diffusion = 0.8
 MESH = pl.DeviceIdType.MESH
 f32 = jnp.float32
@@ -21,7 +22,7 @@
 
 
 def kernel(R, PC, right, blocks, coords, counts, out_x, out_r, tile, thi, tlo, uhi, ulo, dcat,
-           dz, dr, fw, fin, bw, rin, part, din, drow, drin, xs, rs,
+           dz, dr, fw, fin, bw, rin, part, din, drow, drin, xs, rs, ds, im,
            s0, s0s, sp1, sp1s, sb, sbs, sf, sfs, srs, srss, sd, sds, se, ses, so, sos):
     r = lax.axis_index("row")
     c = lax.axis_index("col")
@@ -131,13 +132,11 @@
 
     def stream(ch):
         first[ch].wait_recv()
-        send_p1(0, ch)
         start = dz[0, ch, :, own, :]
-        rs[ch] = start
         xs[ch] = jnp.zeros_like(start)
         reduce_start(0, ch, fold(start * start))
+        send_p1(0, ch)
         yield
-        reduce_middle(0, ch)
         rr = None
         for it in range(ITERS):
             for j in range(R):
@@ -154,6 +153,7 @@
             multiply(thi, tlo, dz[it, ch].reshape(group, cw), fw.at[it, ch])
             for j in range(R):
                 inward(it, ch, lax.rem(r - j + R, R), j, outermost)
+            reduce_middle(2 * it, ch)
             yield
             for tick in range(R + 1):
                 if tick < R:
@@ -180,8 +180,6 @@
                               srs.at[it, ch, j], (to, c))
                 copy.start()
                 drain.append((None, copy))
-            if it == 0:
-                rr = column_sum(reduce_end(0, ch))
             yield
             total = bw[it, ch, :, own, :]
             for j in range(1, R):
@@ -189,24 +187,28 @@
                 total = total + rin[it, ch, j]
             way = dz[it, ch, :, own, :]
             image = way - diffusion * total
-            bw[it, ch, :, own, :] = image
+            norm = column_sum(reduce_end(2 * it, ch))
+            if it > 0:
+                beta = (norm / rr)[None]
+                way = way + beta * ds[ch]
+                image = image + beta * im[ch]
+            rr = norm
+            ds[ch] = way
+            im[ch] = image
             reduce_start(2 * it + 1, ch, fold(way * image))
             yield
             reduce_middle(2 * it + 1, ch)
             yield
             alpha = (rr / column_sum(reduce_end(2 * it + 1, ch)))[None]
-            xs[ch] = xs[ch] + alpha * way
-            residual = rs[ch] - alpha * bw[it, ch, :, own, :]
-            rs[ch] = residual
+            residual = dz[it, ch, :, own, :] - alpha * im[ch]
             if it + 1 < ITERS:
+                dz[it + 1, ch, :, own, :] = residual
                 reduce_start(2 * it + 2, ch, fold(residual * residual))
-                yield
-                reduce_middle(2 * it + 2, ch)
-                yield
-                new = column_sum(reduce_end(2 * it + 2, ch))
-                dz[it + 1, ch, :, own, :] = rs[ch] + (new / rr)[None] * dz[it, ch, :, own, :]
-                rr = new
                 send_p1(it + 1, ch)
+            else:
+                rs[ch] = residual
+            xs[ch] = xs[ch] + alpha * ds[ch]
+            if it + 1 < ITERS:
                 yield
         for n, (kept, out) in enumerate(((xs, out_x), (rs, out_r))):
             out[0, :, columns(a, ch)] = kept[ch, a]
@@ -283,6 +285,8 @@
     half.start()
     drain.append((None, half))
     alive = list(streams)
+    for _ in range(LEAD):
+        next(streams[0])
     while alive:
         for item in list(alive):
             try:
@@ -315,6 +319,7 @@
         vm((ITERS, CHUNKS, R, 2, sh, cw), f32),
         vm((N, CHUNKS, 8, cw), f32), vm((N, CHUNKS, R, 8, cw), f32),
         vm((N, CHUNKS, 8, cw), f32), vm((N, CHUNKS, PC, 8, cw), f32),
+        vm((CHUNKS, 2, sh, cw), f32), vm((CHUNKS, 2, sh, cw), f32),
         vm((CHUNKS, 2, sh, cw), f32), vm((CHUNKS, 2, sh, cw), f32),
         dma((CHUNKS + 1,)), dma((CHUNKS + 1,)),
         dma((ITERS, CHUNKS, R)), dma((ITERS, CHUNKS, R)),

time: 211 us -> 207 us (0.981)
  Pallas kernels: 205 us -> 201 us
    pallas_call x1, Pallas kernels: 205 us -> 201 us  [shards(): pl.pallas_call(functools.partial(kernel, R, PC), out_shape=(out, out), in...]
where the time goes in v4:
time: 207 us
  Pallas kernels  201 us (97%)
  local copies, waits for them, and re-layouts  5.08 us (2%)
    pallas_call x1, Pallas kernels, shards(): pl.pallas_call(functools.partial(kernel, R, PC), out_shape=(out, out), in...  201 us
    unnamed x6, local copies, waits for them, and re-layouts  5.08 us

profile of v4, /device:TPU:1, one launch (start us, length us, event | category | flops | bytes accessed | tf_op | source)
XLA Modules:
  0.0 206.5 jit_solution(2176718107822774225)
XLA Ops:
  0.6 1.3 copy.7.counts
  1.9 1.4 copy.6.coords
  3.3 200.8 %shard_map.59 = (f32[1,128,512]{2,1,0:T(8,128)}, f32[1,128,512]{2,1,0:T(8,128)}) custom-call(f32[1,128,512]{2,1,0:T(8,128)} %right.1, f32[2,1,8,128,128]{4,3,2,1,0:T(8,128)} %blocks.1, s32[2,1,8,2]{3,2,1,0:T(8,128)} %copy.6.coords, s32[2,1]{1,0:T(2,128)} %copy.7.counts), custom_call_target="tpu_custom_call" | custom-call | tf_op jit(solution)/shard_map/pallas_call | solution.py:336
  204.1 0.0 copy-start
  204.1 1.7 copy.10
  205.8 0.0 copy-done
  205.8 0.7 copy.11
Async XLA Ops:
  204.1 1.7 copy-start

commit v5 on v4

--- a/solution.py
+++ b/solution.py
@@ -9,7 +9,7 @@
 
 ITERS = 3
 CHUNKS = 2
-LEAD = 3
+LEAD = 0
 diffusion = 0.8
 MESH = pl.DeviceIdType.MESH
 f32 = jnp.float32
@@ -162,6 +162,8 @@
                 if tick > 0:
                     pl.when(near)(functools.partial(inward_step, it, ch, tick - 1))
                     pl.when(far)(functools.partial(outward_step, it, ch, tick - 1))
+                if it == 0 and ch == CHUNKS - 1 and tick < R:
+                    transpose_part(tick)
                 yield
             for j in range(R):
                 slot = lax.rem(r - j + R, R)
@@ -257,20 +259,33 @@
         pl.when(up)(relay_copy(it, ch, slot, j, 0).start)
         pl.when(down)(relay_copy(it, ch, slot, j, 1).start)
 
+    def split_half(core):
+        @pl.loop(0, group // blk)
+        def _(i):
+            rows = pl.ds(pl.multiple_of(i * blk, blk), blk)
+            cols = pl.ds(pl.multiple_of(core * edge, edge), edge)
+            thi[rows, cols], tlo[rows, cols] = split(tile[core, rows, :])
+
     def prepare():
-        half.wait_recv()
-
-        @pl.loop(0, group // blk)
+        split_half(a)
+        for copy in halves:
+            copy.wait_recv()
+        split_half(1 - a)
+
+    def transpose_part(tick):
+        count = group // blk // R
+
+        @pl.loop(tick * count, (tick + 1) * count)
         def _(i):
             rows = pl.ds(pl.multiple_of(i * blk, blk), blk)
             for u in range(group // blk):
                 piece = tile[u * blk // edge, rows, u * blk % edge:u * blk % edge + blk]
-                thi[rows, u * blk:(u + 1) * blk], tlo[rows, u * blk:(u + 1) * blk] = split(piece)
                 uhi[u * blk:(u + 1) * blk, rows], ulo[u * blk:(u + 1) * blk, rows] = split(piece.T)
 
     streams = [stream(ch) for ch in range(CHUNKS)]
     for item in streams:
         next(item)
+    halves = []
     for m in range(2):
         @pl.loop(0, bt * bt)
         def _(q, m=m):
@@ -281,9 +296,11 @@
                 live = (k < counts[m, 0]) & (coords[m, 0, k, 0] == t) & (coords[m, 0, k, 1] == u)
                 total = total + jnp.where(live, 1.0, 0.0).astype(f32) * blocks[m, 0, k]
             tile[a, pl.ds(pl.multiple_of(m * edge + t * blk, blk), blk), pl.ds(pl.multiple_of(u * blk, blk), blk)] = total
-    half = remote(tile.at[a], tile.at[a], s0s.at[CHUNKS], s0.at[CHUNKS], sibling)
-    half.start()
-    drain.append((None, half))
+        band = tile.at[a, pl.ds(m * edge, edge), :]
+        copy = remote(band, band, s0s.at[CHUNKS + m], s0.at[CHUNKS + m], sibling)
+        copy.start()
+        halves.append(copy)
+        drain.append((None, copy))
     alive = list(streams)
     for _ in range(LEAD):
         next(streams[0])
@@ -321,7 +338,7 @@
         vm((N, CHUNKS, 8, cw), f32), vm((N, CHUNKS, PC, 8, cw), f32),
         vm((CHUNKS, 2, sh, cw), f32), vm((CHUNKS, 2, sh, cw), f32),
         vm((CHUNKS, 2, sh, cw), f32), vm((CHUNKS, 2, sh, cw), f32),
-        dma((CHUNKS + 1,)), dma((CHUNKS + 1,)),
+        dma((CHUNKS + 2,)), dma((CHUNKS + 2,)),
         dma((ITERS, CHUNKS, R)), dma((ITERS, CHUNKS, R)),
         dma((ITERS, CHUNKS, R)), dma((ITERS, CHUNKS, 2, R)),
         dma((ITERS, CHUNKS, 2, R)), dma((ITERS, CHUNKS, R)),

time: 207 us -> 203 us (0.981)
  Pallas kernels: 201 us -> 197 us
    pallas_call x1, Pallas kernels: 201 us -> 197 us  [shards(): pl.pallas_call(functools.partial(kernel, R, PC), out_shape=(out, out), in...]
where the time goes in v5:
time: 203 us; the launch traced here: 202 us
  Pallas kernels  197 us (97%)
  local copies, waits for them, and re-layouts  5.08 us (3%)
    pallas_call x1, Pallas kernels, shards(): pl.pallas_call(functools.partial(kernel, R, PC), out_shape=(out, out), in...  197 us
    unnamed x6, local copies, waits for them, and re-layouts  5.08 us

profile of v5, /device:TPU:1, one launch (start us, length us, event | category | flops | bytes accessed | tf_op | source)
XLA Modules:
  0.0 202.5 jit_solution(5506078204449248319)
XLA Ops:
  0.6 1.3 copy.7.counts
  1.9 1.4 copy.6.coords
  3.3 196.8 %shard_map.59 = (f32[1,128,512]{2,1,0:T(8,128)}, f32[1,128,512]{2,1,0:T(8,128)}) custom-call(f32[1,128,512]{2,1,0:T(8,128)} %right.1, f32[2,1,8,128,128]{4,3,2,1,0:T(8,128)} %blocks.1, s32[2,1,8,2]{3,2,1,0:T(8,128)} %copy.6.coords, s32[2,1]{1,0:T(2,128)} %copy.7.counts), custom_call_target="tpu_custom_call" | custom-call | tf_op jit(solution)/shard_map/pallas_call | solution.py:353
  200.1 0.0 copy-start
  200.1 1.7 copy.10
  201.8 0.0 copy-done
  201.8 0.7 copy.11
Async XLA Ops:
  200.1 1.7 copy-start
